TPU v7x, 32 devices: a whole 2x2x4 slice. The times are simulated.
32 devices in a mesh: samples: 2 (over x), brick: 16 (over z, y, core).
Axes of the slice: x: 2, y: 2, z: 4, core: 2. Of those that a mesh axis runs over, the one named last changes fastest.
Arguments:
- source: float32 [128, 128, 256], P(('samples', 'brick')), parts along dimension 0, may hold values from -6 to 6
- guess: float32 [128, 128, 256], P(('samples', 'brick')), parts along dimension 0, may hold values from -6 to 6
- log_perm: float32 [128, 128, 256], P(('samples', 'brick')), parts along dimension 0, may hold values from -3 to 3
- owner: int32 [16], replicated, may hold values from 0 to 15, each once
Outputs:
- corrected: float32 [128, 128, 256], P(('samples', 'brick')), parts along dimension 0
- coarse_held: float32 [32, 2048], P(('samples', 'brick')), parts along dimension 0
There are 2 independent parts, one for each index of `samples`. A program takes and returns all parts, laid end to end along the dimension named above; an argument that names none is the same for every part. Nothing has to cross between parts.
Inputs may be any that keep to these rules, and one draw needn't show every extreme that they name: `owner`: each brick index appears exactly once.
All inputs are finite; a program needn't handle non-finite values.
Results may differ from a plain program's by a relative error of at most 0.00005.
Values sent between devices are 32-bit elements; how exact they have to be, the bound alone decides.
A program may use at most 64 MiB of HBM per device.

v0:
```python
import jax
import jax.numpy as jnp
from jax import lax
from jax.sharding import PartitionSpec as P

NU = 2
SWEEPS = 8
relax_weight = 0.8


def with_halo(block, sides, width):
    for axis, dim in sides:
        count = lax.axis_size(axis)
        forward = [(i, i + 1) for i in range(count - 1)]
        backward = [(target, source) for source, target in forward]
        low = lax.ppermute(
            lax.slice_in_dim(block, block.shape[dim] - width, None, axis=dim), axis, forward
        )
        high = lax.ppermute(lax.slice_in_dim(block, 0, width, axis=dim), axis, backward)
        block = jnp.concatenate([low, block, high], axis=dim)
    return block


def prolong_matrix(n_fine):
    fine_idx = jnp.arange(n_fine)[:, None]
    coarse_idx = jnp.arange(n_fine // 4)[None, :]
    base = fine_idx // 4
    offset = fine_idx % 4
    weight_own = jnp.where((offset == 0) | (offset == 3), 0.625, 0.875).astype(jnp.float32)
    side = jnp.where(offset < 2, -1, 1)
    own = jnp.where(coarse_idx == base, weight_own, 0.0)
    other = jnp.where(coarse_idx == base + side, 1.0 - weight_own, 0.0)
    return own + other


def local_prolong(planes):
    fine_idx = jnp.arange(planes)[:, None]
    coarse_idx = jnp.arange(planes // 4 + 2)[None, :]
    base = fine_idx // 4 + 1
    offset = fine_idx % 4
    weight_own = jnp.where((offset == 0) | (offset == 3), 0.625, 0.875).astype(jnp.float32)
    side = jnp.where(offset < 2, -1, 1)
    own = jnp.where(coarse_idx == base, weight_own, 0.0)
    other = jnp.where(coarse_idx == base + side, 1.0 - weight_own, 0.0)
    return own + other


def stencil(u_ext, k_ext):
    padded = jnp.pad(u_ext, ((0, 0), (1, 1), (1, 1)))
    kpad = jnp.pad(k_ext, ((0, 0), (1, 1), (1, 1)))
    center = padded[1:-1, 1:-1, 1:-1]
    kcen = kpad[1:-1, 1:-1, 1:-1]
    pairs = [
        (padded[:-2, 1:-1, 1:-1], kpad[:-2, 1:-1, 1:-1]),
        (padded[2:, 1:-1, 1:-1], kpad[2:, 1:-1, 1:-1]),
        (padded[1:-1, :-2, 1:-1], kpad[1:-1, :-2, 1:-1]),
        (padded[1:-1, 2:, 1:-1], kpad[1:-1, 2:, 1:-1]),
        (padded[1:-1, 1:-1, :-2], kpad[1:-1, 1:-1, :-2]),
        (padded[1:-1, 1:-1, 2:], kpad[1:-1, 1:-1, 2:]),
    ]
    diagonal = jnp.zeros_like(center)
    nearby = jnp.zeros_like(center)
    for value, kval in pairs:
        face = 0.5 * (kcen + kval)
        diagonal = diagonal + face
        nearby = nearby + face * value
    return (diagonal * center - nearby, diagonal)


def coarse_apply(field, coeff, zcount):
    columns = field.shape[1]
    zpos = jnp.arange(columns) % zcount
    low_ok = (zpos > 0)[None, :]
    high_ok = (zpos < zcount - 1)[None, :]

    def rows_down(a):
        return jnp.pad(a[:-1], ((1, 0), (0, 0)))

    def rows_up(a):
        return jnp.pad(a[1:], ((0, 1), (0, 0)))

    def cols_down(a, width):
        return jnp.pad(a[:, :-width], ((0, 0), (width, 0)))

    def cols_up(a, width):
        return jnp.pad(a[:, width:], ((0, 0), (0, width)))

    pairs = [
        (rows_down(field), rows_down(coeff)),
        (rows_up(field), rows_up(coeff)),
        (cols_down(field, zcount), cols_down(coeff, zcount)),
        (cols_up(field, zcount), cols_up(coeff, zcount)),
        (jnp.where(low_ok, cols_down(field, 1), 0.0), jnp.where(low_ok, cols_down(coeff, 1), 0.0)),
        (jnp.where(high_ok, cols_up(field, 1), 0.0), jnp.where(high_ok, cols_up(coeff, 1), 0.0)),
    ]
    diagonal = jnp.zeros_like(field)
    nearby = jnp.zeros_like(field)
    for value, kval in pairs:
        face = 0.5 * (coeff + kval)
        diagonal = diagonal + face
        nearby = nearby + face * value
    return (diagonal * field - nearby, diagonal)


def faces(field):
    return with_halo(field, (("brick", 0),), 1)


def local(source, guess, log_perm, owner):
    hp = lax.Precision.HIGHEST
    planes, ny_local, nz_local = source.shape
    cpd = planes // 4
    cyc = ny_local // 4
    czc = nz_local // 4
    cells = cyc * czc
    count = lax.axis_size("brick")
    device = lax.axis_index("brick")
    perm = jnp.exp(log_perm)
    k_ext = with_halo(perm, (("brick", 0),), 1)
    smooth = guess
    for sweep in range(NU):
        image, diagonal = stencil(faces(smooth), k_ext)
        smooth = smooth + relax_weight * (source - image) / diagonal
    image, diagonal = stencil(faces(smooth), k_ext)
    resid = source - image
    py = prolong_matrix(ny_local)
    pz = prolong_matrix(nz_local)
    p_local = local_prolong(planes)
    step_one = jnp.einsum("xyz,yY->xYz", resid, py, precision=hp)
    step_two = jnp.einsum("xYz,zZ->xYZ", step_one, pz, precision=hp)
    partial_value = jnp.einsum("xYZ,xj->jYZ", step_two, p_local, precision=hp) * (1.0 / 64.0)
    partial_value = partial_value.reshape(cpd + 2, cells)
    coarse_own = perm.reshape(cpd, 4, cyc, 4, czc, 4).sum(axis=(1, 3, 5)) * (1.0 / 64.0)
    coarse_own = coarse_own.reshape(cpd, cells)
    middle = partial_value[1 : cpd + 1]
    has_prev = device > 0
    has_next = device < count - 1
    filler = jnp.zeros((cpd - 1, cells), jnp.float32)
    lower_part = jnp.concatenate([filler, partial_value[0:1]], axis=0)
    upper_part = jnp.concatenate([partial_value[cpd + 1 :], filler], axis=0)
    block_ids = jnp.arange(count)[:, None, None]
    self_dest = jnp.take(owner, device)
    prev_dest = jnp.take(owner, jnp.clip(device - 1, 0, count - 1))
    next_dest = jnp.take(owner, jnp.clip(device + 1, 0, count - 1))
    buffer = jnp.where(block_ids == self_dest, middle[None], 0.0)
    buffer = buffer + jnp.where((block_ids == prev_dest) & has_prev, lower_part[None], 0.0)
    buffer = buffer + jnp.where((block_ids == next_dest) & has_next, upper_part[None], 0.0)
    held_rhs = lax.psum_scatter(buffer, "brick", scatter_dimension=0, tiled=True)
    gathered_rhs, coarse_perm = (
        lax.all_gather(held_rhs.reshape(cpd, cells), "brick", axis=0, tiled=True),
        lax.all_gather(coarse_own, "brick", axis=0, tiled=True),
    )
    coarse_rhs = jnp.take(gathered_rhs.reshape(count, cpd, cells), owner, axis=0).reshape(
        count * cpd, cells
    )
    coarse = jnp.zeros_like(coarse_rhs)
    for sweep in range(SWEEPS):
        image, diagonal = coarse_apply(coarse, coarse_perm, czc)
        coarse = coarse + relax_weight * (coarse_rhs - image * (1.0 / 16.0)) / (
            diagonal * (1.0 / 16.0)
        )
    coarse_pad = jnp.pad(coarse, ((1, 1), (0, 0)))
    near_planes = lax.dynamic_slice_in_dim(coarse_pad, device * cpd, cpd + 2, 0).reshape(
        cpd + 2, cyc, czc
    )
    back_one = jnp.einsum("jYZ,xj->xYZ", near_planes, p_local, precision=hp)
    back_two = jnp.einsum("xYZ,yY->xyZ", back_one, py, precision=hp)
    correction = jnp.einsum("xyZ,zZ->xyz", back_two, pz, precision=hp)
    corrected = smooth + correction
    my_block = jnp.sum(jnp.where(owner == device, jnp.arange(count), 0))
    coarse_held = lax.dynamic_slice_in_dim(coarse, my_block * cpd, cpd, 0)
    return (corrected, coarse_held)


def solution(mesh):
    placed = (
        P(("samples", "brick"), None, None),
        P(("samples", "brick"), None, None),
        P(("samples", "brick"), None, None),
        P(),
    )
    return jax.shard_map(
        local,
        mesh=mesh,
        in_specs=placed,
        out_specs=(P(("samples", "brick"), None, None), P(("samples", "brick"), None)),
        check_vma=False,
    )
```

profile of v0, /device:TPU:0, one launch (start us, length us, event | category | flops | bytes accessed | tf_op | source)
XLA Modules:
  0.0 212.1 jit_solution(589605700976618355)
XLA Ops:
  7.2 1.2 exponential_reduce_fusion
  8.4 2.4 %collective-permute-start = (f32[1,128,256]{2,1,0:T(8,128)S(1)}, f32[1,128,256]{2,1,0:T(8,128)S(1)}, u32[]{:S(2)}, u32[]{:S(2)}) collective-permute-start(f32[1,128,256]{2,1,0:T(8,128)S(1)} %get-tuple-element.52), channel_id=1, source_target_pairs={{0,1},{1,2},{2,3},{3,4},{4,5},{5,6},{6,7},{7,8},{8,9},{9,10},{10,1... | collective-permute-start | bytes 393224 | tf_op jit(solution)/shard_map/ppermute | solution.py:16
  10.8 1.3 collective-permute-start.1
  12.1 5.8 %collective-permute-start.2 = (f32[1,128,256]{2,1,0:T(8,128)S(1)}, f32[1,128,256]{2,1,0:T(8,128)}, u32[]{:S(2)}, u32[]{:S(2)}) collective-permute-start(f32[1,128,256]{2,1,0:T(8,128)S(1)} %get-tuple-element.53), channel_id=1, source_target_pairs={{0,1},{1,2},{2,3},{3,4},{4,5},{5,6},{6,7},{7,8},{8,9},{9,10},{10,1... | collective-permute-start | bytes 393224 | tf_op jit(solution)/shard_map/ppermute | solution.py:16
  18.0 1.3 collective-permute-start.3
  19.3 5.7 %reduce_sum.26 = f32[32,4,64,4]{3,2,1,0:T(8,128)} reshape(f32[128,256]{1,0:T(8,128)S(1)} %get-tuple-element.45) | data formatting | bytes 262144 | tf_op jit(solution)/shard_map/reduce_sum | solution.py:133
  25.0 2.5 %reduce_sum.27 = f32[32,64]{1,0:T(8,128)S(1)} reduce(f32[32,4,64,4]{3,2,1,0:T(8,128)} %reduce_sum.26, f32[]{:T(128)} %constant.184.clone.1), dimensions={1,3}, to_apply=%region_2.3 | reduce | flops 30720 | bytes 139268 | tf_op jit(solution)/shard_map/reduce_sum | solution.py:133
  27.6 23.8 %all-gather.1 = f32[16,1,2048]{2,1,0:T(1,128)S(1)} all-gather(f32[1,1,2048]{2,1,0:T(1,128)S(1)} %reshape.582), channel_id=1, replica_groups=mesh['samples'=2,'brick'=16] {'brick'}, dimensions={0}, use_global_device_ids=true | all-gather | bytes 139264 | tf_op jit(solution)/shard_map/all_gather | solution.py:151
  52.4 0.8 fusion.149
  53.8 0.8 copy_bitcast_fusion
  57.8 1.3 select_maximum_fusion.6
  59.8 1.3 select_maximum_fusion.4
  61.2 2.2 %fusion.37 = f32[4,128,256]{2,1,0:T(8,128)S(1)} fusion(f32[4,128,256]{2,1,0:T(8,128)S(1)} %copy-done, f32[4,128,256]{2,1,0:T(8,128)S(1)} %copy-done.1, f32[6,130,258]{2,1,0:T(8,128)S(1)} %select_maximum_fusion.4, f32[1,128,256]{2,1,0:T(8,128)} %copy-done.11, f32[1,128,256]{2,1,0:T(8,128)} %collective-permute-done.2, ...), kind=kLoop, calls=%fused_computation.61 | loop fusion | flops 4980736 | bytes 6815744 | tf_op jit(solution)/shard_map/add | solution.py:123
  63.4 2.3 %collective-permute-start.4 = (f32[1,128,256]{2,1,0:T(8,128)S(1)}, f32[1,128,256]{2,1,0:T(8,128)S(1)}, u32[]{:S(2)}, u32[]{:S(2)}) collective-permute-start(f32[1,128,256]{2,1,0:T(8,128)S(1)} %get-tuple-element.49), channel_id=1, source_target_pairs={{0,1},{1,2},{2,3},{3,4},{4,5},{5,6},{6,7},{7,8},{8,9},{9,10},{10,1... | collective-permute-start | bytes 393224 | tf_op jit(solution)/shard_map/ppermute | solution.py:16
  65.6 1.3 collective-permute-start.5
  67.5 1.3 collective-permute-done.5
  70.0 2.2 %fusion.25 = f32[4,128,256]{2,1,0:T(8,128)S(1)} fusion(f32[4,128,256]{2,1,0:T(8,128)S(1)} %fusion.37, f32[4,128,256]{2,1,0:T(8,128)S(1)} %copy-done.1, f32[6,130,258]{2,1,0:T(8,128)S(1)} %select_maximum_fusion.2, f32[1,128,256]{2,1,0:T(8,128)} %copy-done.13, f32[1,128,256]{2,1,0:T(8,128)} %copy-done.12, f32[4,128,256]{2,1,0:T(8,128)S(1)} %get-tuple-element.46, ...), kind=kLoop, calls=%fused_computation.43 | loop fusion | flops 4980736 | bytes 6815744 | tf_op jit(solution)/shard_map/add | solution.py:123
  72.9 5.0 %collective-permute-start.6 = (f32[1,128,256]{2,1,0:T(8,128)}, f32[1,128,256]{2,1,0:T(8,128)S(1)}, u32[]{:S(2)}, u32[]{:S(2)}) collective-permute-start(f32[1,128,256]{2,1,0:T(8,128)} %get-tuple-element.47), channel_id=1, source_target_pairs={{0,1},{1,2},{2,3},{3,4},{4,5},{5,6},{6,7},{7,8},{8,9},{9,10},{10,1... | collective-permute-start | bytes 393224 | tf_op jit(solution)/shard_map/ppermute | solution.py:16
  77.9 1.3 collective-permute-start.7
  82.3 2.4 %convolution_bitcast_fusion = f32[4,32,256]{2,1,0:T(8,128)S(1)} fusion(f32[4,128,256]{2,1,0:T(8,128)S(1)} %copy-done.1, f32[6,130,258]{2,1,0:T(8,128)S(1)} %select_maximum_fusion, f32[1,128,256]{2,1,0:T(8,128)S(1)} %collective-permute-done.7, f32[4,128,256]{2,1,0:T(8,128)S(1)} %fusion.25, f32[1,128,256]{2,1,0:T(8,128)S(1)} %collective-permute-done.6, ...), kind=kOutput, calls=%fused_computation.17 | convolution fusion | flops 54939648 | bytes 6424576 | tf_op jit(solution)/shard_map/xyz,yY->xYz/dot_general | solution.py:129
  86.6 87.5 %all-reduce.62.cloned.1.call-done = f32[16,1,2048]{2,0,1:T(8,128)} async-done(((f32[16,1,2048]{2,0,1:T(8,128)}), f32[16,1,2048]{2,0,1:T(8,128)}) %all-reduce.62.cloned.1.call-update) | async-done | bytes 131088
  174.0 1.4 dynamic-slice_bitcast_fusion
  175.4 22.6 %all-gather = f32[16,1,2048]{2,1,0:T(1,128)S(1)} all-gather(f32[1,1,2048]{2,1,0:T(1,128)S(1)} %dynamic-slice_bitcast_fusion), channel_id=2, replica_groups=mesh['samples'=2,'brick'=16] {'brick'}, dimensions={0}, use_global_device_ids=true | all-gather | bytes 139264 | tf_op jit(solution)/shard_map/all_gather | solution.py:150
  203.2 1.4 convolution_add_fusion
  (116 shorter events, 14.5 us)
Async XLA Ops:
  7.2 4.9 %copy-start = (f32[4,128,256]{2,1,0:T(8,128)S(1)}, f32[4,128,256]{2,1,0:T(8,128)}, u32[]{:S(2)}) copy-start(f32[4,128,256]{2,1,0:T(8,128)} %param.5) | copy-start | bytes 1572868
  7.2 166.9 %all-reduce.62.cloned.1.call-start = ((), (), s32[]{:S(2)}) async-start(), calls=%async_computation | async-start | bytes 262144
  8.4 48.7 %collective-permute-start = (f32[1,128,256]{2,1,0:T(8,128)S(1)}, f32[1,128,256]{2,1,0:T(8,128)S(1)}, u32[]{:S(2)}, u32[]{:S(2)}) collective-permute-start(f32[1,128,256]{2,1,0:T(8,128)S(1)} %get-tuple-element.52), channel_id=1, source_target_pairs={{0,1},{1,2},{2,3},{3,4},{4,5},{5,6},{6,7},{7,8},{8,9},{9,10},{10,1... | collective-permute-start | bytes 393224 | tf_op jit(solution)/shard_map/ppermute | solution.py:16
  10.8 46.4 %collective-permute-start.1 = (f32[1,128,256]{2,1,0:T(8,128)S(1)}, f32[1,128,256]{2,1,0:T(8,128)}, u32[]{:S(2)}, u32[]{:S(2)}) collective-permute-start(f32[1,128,256]{2,1,0:T(8,128)S(1)} %get-tuple-element.51), channel_id=1, source_target_pairs={{1,0},{2,1},{3,2},{4,3},{5,4},{6,5},{7,6},{8,7},{9,8},{10,9},{11,1... | collective-permute-start | bytes 393224 | tf_op jit(solution)/shard_map/ppermute | solution.py:19
  12.1 47.0 %collective-permute-start.2 = (f32[1,128,256]{2,1,0:T(8,128)S(1)}, f32[1,128,256]{2,1,0:T(8,128)}, u32[]{:S(2)}, u32[]{:S(2)}) collective-permute-start(f32[1,128,256]{2,1,0:T(8,128)S(1)} %get-tuple-element.53), channel_id=1, source_target_pairs={{0,1},{1,2},{2,3},{3,4},{4,5},{5,6},{6,7},{7,8},{8,9},{9,10},{10,1... | collective-permute-start | bytes 393224 | tf_op jit(solution)/shard_map/ppermute | solution.py:16
  18.0 41.2 %collective-permute-start.3 = (f32[1,128,256]{2,1,0:T(8,128)S(1)}, f32[1,128,256]{2,1,0:T(8,128)S(1)}, u32[]{:S(2)}, u32[]{:S(2)}) collective-permute-start(f32[1,128,256]{2,1,0:T(8,128)S(1)} %get-tuple-element.54), channel_id=1, source_target_pairs={{1,0},{2,1},{3,2},{4,3},{5,4},{6,5},{7,6},{8,7},{9,8},{10,9},{11,1... | collective-permute-start | bytes 393224 | tf_op jit(solution)/shard_map/ppermute | solution.py:19
  27.5 25.6 %copy-start.14 = (s32[16]{0:T(128)S(1)}, s32[16]{0:T(128)}, u32[]{:S(2)}) copy-start(s32[16]{0:T(128)} %param.7) | copy-start | bytes 196
  59.1 2.0 copy-start.1
  59.1 2.0 copy-start.3
  63.4 4.1 %collective-permute-start.4 = (f32[1,128,256]{2,1,0:T(8,128)S(1)}, f32[1,128,256]{2,1,0:T(8,128)S(1)}, u32[]{:S(2)}, u32[]{:S(2)}) collective-permute-start(f32[1,128,256]{2,1,0:T(8,128)S(1)} %get-tuple-element.49), channel_id=1, source_target_pairs={{0,1},{1,2},{2,3},{3,4},{4,5},{5,6},{6,7},{7,8},{8,9},{9,10},{10,1... | collective-permute-start | bytes 393224 | tf_op jit(solution)/shard_map/ppermute | solution.py:16
  65.6 3.2 %collective-permute-start.5 = (f32[1,128,256]{2,1,0:T(8,128)S(1)}, f32[1,128,256]{2,1,0:T(8,128)S(1)}, u32[]{:S(2)}, u32[]{:S(2)}) collective-permute-start(f32[1,128,256]{2,1,0:T(8,128)S(1)} %get-tuple-element.50), channel_id=1, source_target_pairs={{1,0},{2,1},{3,2},{4,3},{5,4},{6,5},{7,6},{8,7},{9,8},{10,9},{11,1... | collective-permute-start | bytes 393224 | tf_op jit(solution)/shard_map/ppermute | solution.py:19
  67.5 1.4 copy-start.12
  70.0 10.6 %copy-start.15 = (u32[32]{0:T(128)S(1)}, u32[32]{0:T(128)}, u32[]{:S(2)}) copy-start(u32[32]{0:T(128)} %constant.395) | copy-start | bytes 388
  72.2 10.0 %copy-start.4 = (f32[1,128,256]{2,1,0:T(8,128)S(1)}, f32[1,128,256]{2,1,0:T(8,128)}, u32[]{:S(2)}) copy-start(f32[1,128,256]{2,1,0:T(8,128)} %copy-done.2) | copy-start | bytes 393220
  72.9 8.9 %collective-permute-start.6 = (f32[1,128,256]{2,1,0:T(8,128)}, f32[1,128,256]{2,1,0:T(8,128)S(1)}, u32[]{:S(2)}, u32[]{:S(2)}) collective-permute-start(f32[1,128,256]{2,1,0:T(8,128)} %get-tuple-element.47), channel_id=1, source_target_pairs={{0,1},{1,2},{2,3},{3,4},{4,5},{5,6},{6,7},{7,8},{8,9},{9,10},{10,1... | collective-permute-start | bytes 393224 | tf_op jit(solution)/shard_map/ppermute | solution.py:16
  77.9 4.0 %collective-permute-start.7 = (f32[1,128,256]{2,1,0:T(8,128)S(1)}, f32[1,128,256]{2,1,0:T(8,128)S(1)}, u32[]{:S(2)}, u32[]{:S(2)}) collective-permute-start(f32[1,128,256]{2,1,0:T(8,128)S(1)} %get-tuple-element.48), channel_id=1, source_target_pairs={{1,0},{2,1},{3,2},{4,3},{5,4},{6,5},{7,6},{8,7},{9,8},{10,9},{11,1... | collective-permute-start | bytes 393224 | tf_op jit(solution)/shard_map/ppermute | solution.py:19
  82.2 2.7 %copy-start.16 = (s32[4]{0:T(128)S(1)}, s32[4]{0:T(128)}, u32[]{:S(2)}) copy-start(s32[4]{0:T(128)} %get-tuple-element.114) | copy-start | bytes 52
  82.3 2.7 %copy-start.17 = (s32[4]{0:T(128)S(1)}, s32[4]{0:T(128)}, u32[]{:S(2)}) copy-start(s32[4]{0:T(128)} %get-tuple-element.115) | copy-start | bytes 52
  85.3 113.4 %copy-start.5 = (f32[16,1984]{1,0:T(8,128)S(1)}, f32[16,1984]{1,0:T(8,128)}, u32[]{:S(2)}) copy-start(f32[16,1984]{1,0:T(8,128)} %get-tuple-element.99) | copy-start | bytes 380932
  85.4 113.4 %copy-start.6 = (f32[16,1984]{1,0:T(8,128)S(1)}, f32[16,1984]{1,0:T(8,128)}, u32[]{:S(2)}) copy-start(f32[16,1984]{1,0:T(8,128)} %get-tuple-element.100) | copy-start | bytes 380932
  85.4 113.4 %copy-start.7 = (f32[16,2047]{1,0:T(8,128)S(1)}, f32[16,2047]{1,0:T(8,128)}, u32[]{:S(2)}) copy-start(f32[16,2047]{1,0:T(8,128)} %get-tuple-element.97) | copy-start | bytes 393028
  85.4 113.4 %copy-start.8 = (f32[16,2047]{1,0:T(8,128)S(1)}, f32[16,2047]{1,0:T(8,128)}, u32[]{:S(2)}) copy-start(f32[16,2047]{1,0:T(8,128)} %get-tuple-element.98) | copy-start | bytes 393028
  85.4 113.4 %copy-start.9 = (f32[15,2048]{1,0:T(8,128)S(1)}, f32[15,2048]{1,0:T(8,128)}, u32[]{:S(2)}) copy-start(f32[15,2048]{1,0:T(8,128)} %get-tuple-element.122) | copy-start | bytes 368644
  85.4 113.4 %copy-start.10 = (f32[15,2048]{1,0:T(8,128)S(1)}, f32[15,2048]{1,0:T(8,128)}, u32[]{:S(2)}) copy-start(f32[15,2048]{1,0:T(8,128)} %get-tuple-element.123) | copy-start | bytes 368644
  (3 other events, 2.0 us)
Sparse Core Ops, SparseCore 0:
  86.7 87.3 all-reduce.61
where the time goes:
time: 213 us; the launch traced here: 212 us
  waiting for transfers between devices  88.9 us (42%)
  blocking collectives  46.4 us (22%)
  starting transfers between devices  20.6 us (10%)
  between operations  18.7 us (9%)
  local copies, waits for them, and re-layouts  16.8 us (8%)
  other arithmetic  15.6 us (7%)
  matrix products  5.18 us (2%)
    unnamed x2, waiting for transfers between devices  87.5 us
    all_gather x1, blocking collectives, local(): lax.all_gather(coarse_own, 'brick', axis=0, tiled=True)  23.8 us
    all_gather x1, blocking collectives, local(): lax.all_gather(held_rhs.reshape(cpd, cells), 'brick', axis=0, tiled=True)  22.6 us
    ppermute x4, starting transfers between devices, with_halo(): lax.ppermute(lax.slice_in_dim(block, block.shape[dim] - width, None, axis...  15.4 us
    reduce_sum x1, local copies, waits for them, and re-layouts, local(): perm.reshape(cpd, 4, cyc, 4, czc, 4).sum(axis=(1, 3, 5)) * (1.0 / 64.0)  5.67 us
    ppermute x4, starting transfers between devices, with_halo(): lax.ppermute(lax.slice_in_dim(block, 0, width, axis=dim), axis, backward)  5.16 us
    add x2, other arithmetic, local(): smooth = smooth + relax_weight * (source - image) / diagonal  4.4 us
  transfers between devices with their start and end apart: 9, of which 2 were waited for; matrix products, arithmetic and copies ran while one was open for 7% of the time, Pallas kernels for 0%

commit v1 on v0

--- a/solution.py
+++ b/solution.py
@@ -6,6 +6,27 @@
 NU = 2
 SWEEPS = 8
 relax_weight = 0.8
+
+
+def gather_around(x, axis, dim):
+    size, position, rows = (lax.axis_size(axis), lax.axis_index(axis), x.shape[dim])
+    right = [(i, (i + 1) % size) for i in range(size)]
+    left = [(i, (i - 1) % size) for i in range(size)]
+    out = jnp.zeros((*x.shape[:dim], size * rows, *x.shape[dim + 1 :]), x.dtype)
+    out = lax.dynamic_update_slice_in_dim(out, x, position * rows, axis=dim)
+    from_left = from_right = x
+    half = size // 2
+    for step in range(1, half + 1):
+        from_left = lax.ppermute(from_left, axis, right)
+        out = lax.dynamic_update_slice_in_dim(
+            out, from_left, (position - step) % size * rows, axis=dim
+        )
+        if step < size - half:
+            from_right = lax.ppermute(from_right, axis, left)
+            out = lax.dynamic_update_slice_in_dim(
+                out, from_right, (position + step) % size * rows, axis=dim
+            )
+    return out
 
 
 def with_halo(block, sides, width):
@@ -147,7 +168,7 @@
     buffer = buffer + jnp.where((block_ids == next_dest) & has_next, upper_part[None], 0.0)
     held_rhs = lax.psum_scatter(buffer, "brick", scatter_dimension=0, tiled=True)
     gathered_rhs, coarse_perm = (
-        lax.all_gather(held_rhs.reshape(cpd, cells), "brick", axis=0, tiled=True),
+        gather_around(held_rhs.reshape(cpd, cells), "brick", 0),
         lax.all_gather(coarse_own, "brick", axis=0, tiled=True),
     )
     coarse_rhs = jnp.take(gathered_rhs.reshape(count, cpd, cells), owner, axis=0).reshape(

time: 213 us -> 228 us (1.070)
  starting transfers between devices: 20.6 us -> 53.6 us
  blocking collectives: 46.4 us -> 23.1 us
  waiting for transfers between devices: 88.9 us -> 95.8 us
    ppermute x0 -> x15, starting transfers between devices: none -> 31 us  [the longest x7 30.6 us: gather_around(): from_right = lax.ppermute(from_right, axis, left)]
    all_gather x1 -> x0, blocking collectives: 22.6 us -> none  [local(): lax.all_gather(held_rhs.reshape(cpd, cells), 'brick', axis=0, tiled=True)]
    ppermute x0 -> x15, waiting for transfers between devices: none -> 8.71 us  [the longest x8 6.57 us: gather_around(): from_left = lax.ppermute(from_left, axis, right)]
    dynamic_update_slice x0 -> x18, local copies, waits for them, and re-layouts: none -> 4.77 us  [the longest x10 3.13 us: gather_around(): lax.dynamic_update_slice_in_dim(out, from_left, (position - step) % size...]
    unnamed x2, waiting for transfers between devices: 87.5 us -> 84 us
  transfers between devices with their start and end apart: 9 -> 24, of which waited for: 2 -> 15; matrix products, arithmetic and copies ran while one was open for 7% -> 7% of each run, Pallas kernels for 0% -> 0%
where the time goes in v1:
time: 228 us; the launch traced here: 227 us
  waiting for transfers between devices  95.8 us (42%)
  starting transfers between devices  53.6 us (24%)
  blocking collectives  23.1 us (10%)
  between operations  18.9 us (8%)
  local copies, waits for them, and re-layouts  17 us (7%)
  other arithmetic  14.3 us (6%)
  matrix products  4.28 us (2%)
    unnamed x2, waiting for transfers between devices  84 us
    ppermute x7, starting transfers between devices, gather_around(): from_right = lax.ppermute(from_right, axis, left)  30.6 us
    all_gather x1, blocking collectives, local(): lax.all_gather(coarse_own, 'brick', axis=0, tiled=True)  23.1 us
    ppermute x4, starting transfers between devices, with_halo(): lax.ppermute(lax.slice_in_dim(block, block.shape[dim] - width, None, axis...  17.4 us
    ppermute x8, waiting for transfers between devices, gather_around(): from_left = lax.ppermute(from_left, axis, right)  6.57 us
    reduce_sum x1, local copies, waits for them, and re-layouts, local(): perm.reshape(cpd, 4, cyc, 4, czc, 4).sum(axis=(1, 3, 5)) * (1.0 / 64.0)  5.7 us
    ppermute x4, starting transfers between devices, with_halo(): lax.ppermute(lax.slice_in_dim(block, 0, width, axis=dim), axis, backward)  5.16 us
  transfers between devices with their start and end apart: 24, of which 15 were waited for; matrix products, arithmetic and copies ran while one was open for 7% of the time, Pallas kernels for 0%

profile of v1, /device:TPU:0, one launch (start us, length us, event | category | flops | bytes accessed | tf_op | source)
XLA Modules:
  0.0 227.0 jit_solution(10426810684633416479)
XLA Ops:
  8.4 2.4 %collective-permute-start = (f32[1,128,256]{2,1,0:T(8,128)S(1)}, f32[1,128,256]{2,1,0:T(8,128)S(1)}, u32[]{:S(2)}, u32[]{:S(2)}) collective-permute-start(f32[1,128,256]{2,1,0:T(8,128)S(1)} %get-tuple-element.52), channel_id=1, source_target_pairs={{0,1},{1,2},{2,3},{3,4},{4,5},{5,6},{6,7},{7,8},{8,9},{9,10},{10,1... | collective-permute-start | bytes 393224 | tf_op jit(solution)/shard_map/ppermute | solution.py:37
  10.8 1.3 collective-permute-start.1
  12.8 5.8 %collective-permute-start.2 = (f32[1,128,256]{2,1,0:T(8,128)}, f32[1,128,256]{2,1,0:T(8,128)}, u32[]{:S(2)}, u32[]{:S(2)}) collective-permute-start(f32[1,128,256]{2,1,0:T(8,128)} %get-tuple-element.53), channel_id=1, source_target_pairs={{0,1},{1,2},{2,3},{3,4},{4,5},{5,6},{6,7},{7,8},{8,9},{9,10},{10,1... | collective-permute-start | bytes 393224 | tf_op jit(solution)/shard_map/ppermute | solution.py:37
  20.0 5.7 %reduce_sum.26 = f32[32,4,64,4]{3,2,1,0:T(8,128)} reshape(f32[128,256]{1,0:T(8,128)S(1)} %get-tuple-element.45) | data formatting | bytes 262144 | tf_op jit(solution)/shard_map/reduce_sum | solution.py:154
  25.7 2.6 %reduce_sum.27 = f32[32,64]{1,0:T(8,128)S(1)} reduce(f32[32,4,64,4]{3,2,1,0:T(8,128)} %reduce_sum.26, f32[]{:T(128)} %constant.278.clone.1), dimensions={1,3}, to_apply=%region_2.3 | reduce | flops 30720 | bytes 139268 | tf_op jit(solution)/shard_map/reduce_sum | solution.py:154
  31.6 1.4 select_maximum_fusion.4
  33.0 2.2 fusion.37
  35.2 3.6 %collective-permute-start.4 = (f32[1,128,256]{2,1,0:T(8,128)S(1)}, f32[1,128,256]{2,1,0:T(8,128)S(1)}, u32[]{:S(2)}, u32[]{:S(2)}) collective-permute-start(f32[1,128,256]{2,1,0:T(8,128)S(1)} %get-tuple-element.49), channel_id=1, source_target_pairs={{0,1},{1,2},{2,3},{3,4},{4,5},{5,6},{6,7},{7,8},{8,9},{9,10},{10,1... | collective-permute-start | bytes 393224 | tf_op jit(solution)/shard_map/ppermute | solution.py:37
  38.9 1.3 collective-permute-start.5
  40.3 3.0 %collective-permute-done.5 = f32[1,128,256]{2,1,0:T(8,128)S(1)} collective-permute-done((f32[1,128,256]{2,1,0:T(8,128)S(1)}, f32[1,128,256]{2,1,0:T(8,128)S(1)}, u32[]{:S(2)}, u32[]{:S(2)}) %collective-permute-start.5) | collective-permute-done | bytes 131104 | tf_op jit(solution)/shard_map/ppermute | solution.py:40
  44.4 2.2 fusion.25
  46.7 5.6 %collective-permute-start.6 = (f32[1,128,256]{2,1,0:T(8,128)S(1)}, f32[1,128,256]{2,1,0:T(8,128)S(1)}, u32[]{:S(2)}, u32[]{:S(2)}) collective-permute-start(f32[1,128,256]{2,1,0:T(8,128)S(1)} %get-tuple-element.47), channel_id=1, source_target_pairs={{0,1},{1,2},{2,3},{3,4},{4,5},{5,6},{6,7},{7,8},{8,9},{9,10},{10,1... | collective-permute-start | bytes 393224 | tf_op jit(solution)/shard_map/ppermute | solution.py:37
  53.6 23.1 %all-gather = f32[16,1,2048]{2,1,0:T(1,128)S(1)} all-gather(f32[1,1,2048]{2,1,0:T(1,128)S(1)} %reshape.704), channel_id=1, replica_groups=mesh['samples'=2,'brick'=16] {'brick'}, dimensions={0}, use_global_device_ids=true | all-gather | bytes 139264 | tf_op jit(solution)/shard_map/all_gather | solution.py:172
  77.1 1.5 convolution_bitcast_fusion
  81.3 84.0 %all-reduce.62.cloned.1.call-done = f32[16,1,2048]{2,1,0:T(1,128)} async-done(((f32[16,1,2048]{2,1,0:T(1,128)}), f32[16,1,2048]{2,1,0:T(1,128)}) %all-reduce.62.cloned.1.call-update) | async-done | bytes 131088
  165.4 1.3 dynamic-slice_bitcast_fusion
  167.2 4.2 %collective-permute-start.9 = (f32[1,2048]{1,0:T(1,128)S(1)}, f32[1,2048]{1,0:T(1,128)S(1)}, u32[]{:S(2)}, u32[]{:S(2)}) collective-permute-start(f32[1,2048]{1,0:T(1,128)S(1)} %dynamic-slice_bitcast_fusion), channel_id=1, source_target_pairs={{0,15},{1,0},{2,1},{3,2},{4,3},{5,4},{6,5},{7,6},{8,7},{9,8},{10,9... | collective-permute-start | bytes 24584 | tf_op jit(solution)/shard_map/ppermute | solution.py:25
  172.7 4.4 %collective-permute-start.11 = (f32[1,2048]{1,0:T(1,128)S(1)}, f32[1,2048]{1,0:T(1,128)S(1)}, u32[]{:S(2)}, u32[]{:S(2)}) collective-permute-start(f32[1,2048]{1,0:T(1,128)S(1)} %collective-permute-done.9), channel_id=1, source_target_pairs={{0,15},{1,0},{2,1},{3,2},{4,3},{5,4},{6,5},{7,6},{8,7},{9,8},{10,9... | collective-permute-start | bytes 24584 | tf_op jit(solution)/shard_map/ppermute | solution.py:25
  178.5 4.4 %collective-permute-start.13 = (f32[1,2048]{1,0:T(1,128)S(1)}, f32[1,2048]{1,0:T(1,128)S(1)}, u32[]{:S(2)}, u32[]{:S(2)}) collective-permute-start(f32[1,2048]{1,0:T(1,128)S(1)} %collective-permute-done.11), channel_id=1, source_target_pairs={{0,15},{1,0},{2,1},{3,2},{4,3},{5,4},{6,5},{7,6},{8,7},{9,8},{10,9... | collective-permute-start | bytes 24584 | tf_op jit(solution)/shard_map/ppermute | solution.py:25
  184.7 4.4 %collective-permute-start.15 = (f32[1,2048]{1,0:T(1,128)S(1)}, f32[1,2048]{1,0:T(1,128)S(1)}, u32[]{:S(2)}, u32[]{:S(2)}) collective-permute-start(f32[1,2048]{1,0:T(1,128)S(1)} %collective-permute-done.13), channel_id=1, source_target_pairs={{0,15},{1,0},{2,1},{3,2},{4,3},{5,4},{6,5},{7,6},{8,7},{9,8},{10,9... | collective-permute-start | bytes 24584 | tf_op jit(solution)/shard_map/ppermute | solution.py:25
  190.5 4.4 %collective-permute-start.17 = (f32[1,2048]{1,0:T(1,128)S(1)}, f32[1,2048]{1,0:T(1,128)S(1)}, u32[]{:S(2)}, u32[]{:S(2)}) collective-permute-start(f32[1,2048]{1,0:T(1,128)S(1)} %collective-permute-done.15), channel_id=1, source_target_pairs={{0,15},{1,0},{2,1},{3,2},{4,3},{5,4},{6,5},{7,6},{8,7},{9,8},{10,9... | collective-permute-start | bytes 24584 | tf_op jit(solution)/shard_map/ppermute | solution.py:25
  196.3 4.4 %collective-permute-start.19 = (f32[1,2048]{1,0:T(1,128)S(1)}, f32[1,2048]{1,0:T(1,128)S(1)}, u32[]{:S(2)}, u32[]{:S(2)}) collective-permute-start(f32[1,2048]{1,0:T(1,128)S(1)} %collective-permute-done.17), channel_id=1, source_target_pairs={{0,15},{1,0},{2,1},{3,2},{4,3},{5,4},{6,5},{7,6},{8,7},{9,8},{10,9... | collective-permute-start | bytes 24584 | tf_op jit(solution)/shard_map/ppermute | solution.py:25
  202.0 4.4 %collective-permute-start.21 = (f32[1,2048]{1,0:T(1,128)S(1)}, f32[1,2048]{1,0:T(1,128)S(1)}, u32[]{:S(2)}, u32[]{:S(2)}) collective-permute-start(f32[1,2048]{1,0:T(1,128)S(1)} %collective-permute-done.19), channel_id=1, source_target_pairs={{0,15},{1,0},{2,1},{3,2},{4,3},{5,4},{6,5},{7,6},{8,7},{9,8},{10,9... | collective-permute-start | bytes 24584 | tf_op jit(solution)/shard_map/ppermute | solution.py:25
  218.2 1.4 convolution_add_fusion
  (141 shorter events, 29.1 us)
Async XLA Ops:
  7.2 158.2 %all-reduce.62.cloned.1.call-start = ((), (), s32[]{:S(2)}) async-start(), calls=%async_computation | async-start | bytes 262144
  8.4 22.5 %collective-permute-start = (f32[1,128,256]{2,1,0:T(8,128)S(1)}, f32[1,128,256]{2,1,0:T(8,128)S(1)}, u32[]{:S(2)}, u32[]{:S(2)}) collective-permute-start(f32[1,128,256]{2,1,0:T(8,128)S(1)} %get-tuple-element.52), channel_id=1, source_target_pairs={{0,1},{1,2},{2,3},{3,4},{4,5},{5,6},{6,7},{7,8},{8,9},{9,10},{10,1... | collective-permute-start | bytes 393224 | tf_op jit(solution)/shard_map/ppermute | solution.py:37
  10.8 20.2 %collective-permute-start.1 = (f32[1,128,256]{2,1,0:T(8,128)S(1)}, f32[1,128,256]{2,1,0:T(8,128)S(1)}, u32[]{:S(2)}, u32[]{:S(2)}) collective-permute-start(f32[1,128,256]{2,1,0:T(8,128)S(1)} %get-tuple-element.51), channel_id=1, source_target_pairs={{1,0},{2,1},{3,2},{4,3},{5,4},{6,5},{7,6},{8,7},{9,8},{10,9},{11,1... | collective-permute-start | bytes 393224 | tf_op jit(solution)/shard_map/ppermute | solution.py:40
  12.8 18.6 %collective-permute-start.2 = (f32[1,128,256]{2,1,0:T(8,128)}, f32[1,128,256]{2,1,0:T(8,128)}, u32[]{:S(2)}, u32[]{:S(2)}) collective-permute-start(f32[1,128,256]{2,1,0:T(8,128)} %get-tuple-element.53), channel_id=1, source_target_pairs={{0,1},{1,2},{2,3},{3,4},{4,5},{5,6},{6,7},{7,8},{8,9},{9,10},{10,1... | collective-permute-start | bytes 393224 | tf_op jit(solution)/shard_map/ppermute | solution.py:37
  18.6 12.8 %collective-permute-start.3 = (f32[1,128,256]{2,1,0:T(8,128)}, f32[1,128,256]{2,1,0:T(8,128)}, u32[]{:S(2)}, u32[]{:S(2)}) collective-permute-start(f32[1,128,256]{2,1,0:T(8,128)} %get-tuple-element.54), channel_id=1, source_target_pairs={{1,0},{2,1},{3,2},{4,3},{5,4},{6,5},{7,6},{8,7},{9,8},{10,9},{11,1... | collective-permute-start | bytes 393224 | tf_op jit(solution)/shard_map/ppermute | solution.py:40
  35.2 5.1 %collective-permute-start.4 = (f32[1,128,256]{2,1,0:T(8,128)S(1)}, f32[1,128,256]{2,1,0:T(8,128)S(1)}, u32[]{:S(2)}, u32[]{:S(2)}) collective-permute-start(f32[1,128,256]{2,1,0:T(8,128)S(1)} %get-tuple-element.49), channel_id=1, source_target_pairs={{0,1},{1,2},{2,3},{3,4},{4,5},{5,6},{6,7},{7,8},{8,9},{9,10},{10,1... | collective-permute-start | bytes 393224 | tf_op jit(solution)/shard_map/ppermute | solution.py:37
  38.9 4.5 %collective-permute-start.5 = (f32[1,128,256]{2,1,0:T(8,128)S(1)}, f32[1,128,256]{2,1,0:T(8,128)S(1)}, u32[]{:S(2)}, u32[]{:S(2)}) collective-permute-start(f32[1,128,256]{2,1,0:T(8,128)S(1)} %get-tuple-element.50), channel_id=1, source_target_pairs={{1,0},{2,1},{3,2},{4,3},{5,4},{6,5},{7,6},{8,7},{9,8},{10,9},{11,1... | collective-permute-start | bytes 393224 | tf_op jit(solution)/shard_map/ppermute | solution.py:40
  46.7 30.0 %collective-permute-start.6 = (f32[1,128,256]{2,1,0:T(8,128)S(1)}, f32[1,128,256]{2,1,0:T(8,128)S(1)}, u32[]{:S(2)}, u32[]{:S(2)}) collective-permute-start(f32[1,128,256]{2,1,0:T(8,128)S(1)} %get-tuple-element.47), channel_id=1, source_target_pairs={{0,1},{1,2},{2,3},{3,4},{4,5},{5,6},{6,7},{7,8},{8,9},{9,10},{10,1... | collective-permute-start | bytes 393224 | tf_op jit(solution)/shard_map/ppermute | solution.py:37
  52.3 24.4 %collective-permute-start.7 = (f32[1,128,256]{2,1,0:T(8,128)S(1)}, f32[1,128,256]{2,1,0:T(8,128)S(1)}, u32[]{:S(2)}, u32[]{:S(2)}) collective-permute-start(f32[1,128,256]{2,1,0:T(8,128)S(1)} %get-tuple-element.48), channel_id=1, source_target_pairs={{1,0},{2,1},{3,2},{4,3},{5,4},{6,5},{7,6},{8,7},{9,8},{10,9},{11,1... | collective-permute-start | bytes 393224 | tf_op jit(solution)/shard_map/ppermute | solution.py:40
  166.7 5.8 %collective-permute-start.8 = (f32[1,2048]{1,0:T(1,128)S(1)}, f32[1,2048]{1,0:T(1,128)S(1)}, u32[]{:S(2)}, u32[]{:S(2)}) collective-permute-start(f32[1,2048]{1,0:T(1,128)S(1)} %dynamic-slice_bitcast_fusion), channel_id=1, source_target_pairs={{0,1},{1,2},{2,3},{3,4},{4,5},{5,6},{6,7},{7,8},{8,9},{9,10},{10,1... | collective-permute-start | bytes 24584 | tf_op jit(solution)/shard_map/ppermute | solution.py:20
  167.2 5.5 %collective-permute-start.9 = (f32[1,2048]{1,0:T(1,128)S(1)}, f32[1,2048]{1,0:T(1,128)S(1)}, u32[]{:S(2)}, u32[]{:S(2)}) collective-permute-start(f32[1,2048]{1,0:T(1,128)S(1)} %dynamic-slice_bitcast_fusion), channel_id=1, source_target_pairs={{0,15},{1,0},{2,1},{3,2},{4,3},{5,4},{6,5},{7,6},{8,7},{9,8},{10,9... | collective-permute-start | bytes 24584 | tf_op jit(solution)/shard_map/ppermute | solution.py:25
  172.5 5.8 %collective-permute-start.10 = (f32[1,2048]{1,0:T(1,128)S(1)}, f32[1,2048]{1,0:T(1,128)S(1)}, u32[]{:S(2)}, u32[]{:S(2)}) collective-permute-start(f32[1,2048]{1,0:T(1,128)S(1)} %collective-permute-done.8), channel_id=1, source_target_pairs={{0,1},{1,2},{2,3},{3,4},{4,5},{5,6},{6,7},{7,8},{8,9},{9,10},{10,1... | collective-permute-start | bytes 24584 | tf_op jit(solution)/shard_map/ppermute | solution.py:20
  172.7 5.8 %collective-permute-start.11 = (f32[1,2048]{1,0:T(1,128)S(1)}, f32[1,2048]{1,0:T(1,128)S(1)}, u32[]{:S(2)}, u32[]{:S(2)}) collective-permute-start(f32[1,2048]{1,0:T(1,128)S(1)} %collective-permute-done.9), channel_id=1, source_target_pairs={{0,15},{1,0},{2,1},{3,2},{4,3},{5,4},{6,5},{7,6},{8,7},{9,8},{10,9... | collective-permute-start | bytes 24584 | tf_op jit(solution)/shard_map/ppermute | solution.py:25
  178.3 5.8 %collective-permute-start.12 = (f32[1,2048]{1,0:T(1,128)S(1)}, f32[1,2048]{1,0:T(1,128)S(1)}, u32[]{:S(2)}, u32[]{:S(2)}) collective-permute-start(f32[1,2048]{1,0:T(1,128)S(1)} %collective-permute-done.10), channel_id=1, source_target_pairs={{0,1},{1,2},{2,3},{3,4},{4,5},{5,6},{6,7},{7,8},{8,9},{9,10},{10,1... | collective-permute-start | bytes 24584 | tf_op jit(solution)/shard_map/ppermute | solution.py:20
  178.5 6.2 %collective-permute-start.13 = (f32[1,2048]{1,0:T(1,128)S(1)}, f32[1,2048]{1,0:T(1,128)S(1)}, u32[]{:S(2)}, u32[]{:S(2)}) collective-permute-start(f32[1,2048]{1,0:T(1,128)S(1)} %collective-permute-done.11), channel_id=1, source_target_pairs={{0,15},{1,0},{2,1},{3,2},{4,3},{5,4},{6,5},{7,6},{8,7},{9,8},{10,9... | collective-permute-start | bytes 24584 | tf_op jit(solution)/shard_map/ppermute | solution.py:25
  184.0 5.8 %collective-permute-start.14 = (f32[1,2048]{1,0:T(1,128)S(1)}, f32[1,2048]{1,0:T(1,128)S(1)}, u32[]{:S(2)}, u32[]{:S(2)}) collective-permute-start(f32[1,2048]{1,0:T(1,128)S(1)} %collective-permute-done.12), channel_id=1, source_target_pairs={{0,1},{1,2},{2,3},{3,4},{4,5},{5,6},{6,7},{7,8},{8,9},{9,10},{10,1... | collective-permute-start | bytes 24584 | tf_op jit(solution)/shard_map/ppermute | solution.py:20
  184.7 5.8 %collective-permute-start.15 = (f32[1,2048]{1,0:T(1,128)S(1)}, f32[1,2048]{1,0:T(1,128)S(1)}, u32[]{:S(2)}, u32[]{:S(2)}) collective-permute-start(f32[1,2048]{1,0:T(1,128)S(1)} %collective-permute-done.13), channel_id=1, source_target_pairs={{0,15},{1,0},{2,1},{3,2},{4,3},{5,4},{6,5},{7,6},{8,7},{9,8},{10,9... | collective-permute-start | bytes 24584 | tf_op jit(solution)/shard_map/ppermute | solution.py:25
  189.8 5.8 %collective-permute-start.16 = (f32[1,2048]{1,0:T(1,128)S(1)}, f32[1,2048]{1,0:T(1,128)S(1)}, u32[]{:S(2)}, u32[]{:S(2)}) collective-permute-start(f32[1,2048]{1,0:T(1,128)S(1)} %collective-permute-done.14), channel_id=1, source_target_pairs={{0,1},{1,2},{2,3},{3,4},{4,5},{5,6},{6,7},{7,8},{8,9},{9,10},{10,1... | collective-permute-start | bytes 24584 | tf_op jit(solution)/shard_map/ppermute | solution.py:20
  190.5 5.8 %collective-permute-start.17 = (f32[1,2048]{1,0:T(1,128)S(1)}, f32[1,2048]{1,0:T(1,128)S(1)}, u32[]{:S(2)}, u32[]{:S(2)}) collective-permute-start(f32[1,2048]{1,0:T(1,128)S(1)} %collective-permute-done.15), channel_id=1, source_target_pairs={{0,15},{1,0},{2,1},{3,2},{4,3},{5,4},{6,5},{7,6},{8,7},{9,8},{10,9... | collective-permute-start | bytes 24584 | tf_op jit(solution)/shard_map/ppermute | solution.py:25
  195.6 5.8 %collective-permute-start.18 = (f32[1,2048]{1,0:T(1,128)S(1)}, f32[1,2048]{1,0:T(1,128)S(1)}, u32[]{:S(2)}, u32[]{:S(2)}) collective-permute-start(f32[1,2048]{1,0:T(1,128)S(1)} %collective-permute-done.16), channel_id=1, source_target_pairs={{0,1},{1,2},{2,3},{3,4},{4,5},{5,6},{6,7},{7,8},{8,9},{9,10},{10,1... | collective-permute-start | bytes 24584 | tf_op jit(solution)/shard_map/ppermute | solution.py:20
  196.3 5.8 %collective-permute-start.19 = (f32[1,2048]{1,0:T(1,128)S(1)}, f32[1,2048]{1,0:T(1,128)S(1)}, u32[]{:S(2)}, u32[]{:S(2)}) collective-permute-start(f32[1,2048]{1,0:T(1,128)S(1)} %collective-permute-done.17), channel_id=1, source_target_pairs={{0,15},{1,0},{2,1},{3,2},{4,3},{5,4},{6,5},{7,6},{8,7},{9,8},{10,9... | collective-permute-start | bytes 24584 | tf_op jit(solution)/shard_map/ppermute | solution.py:25
  201.4 5.8 %collective-permute-start.20 = (f32[1,2048]{1,0:T(1,128)S(1)}, f32[1,2048]{1,0:T(1,128)S(1)}, u32[]{:S(2)}, u32[]{:S(2)}) collective-permute-start(f32[1,2048]{1,0:T(1,128)S(1)} %collective-permute-done.18), channel_id=1, source_target_pairs={{0,1},{1,2},{2,3},{3,4},{4,5},{5,6},{6,7},{7,8},{8,9},{9,10},{10,1... | collective-permute-start | bytes 24584 | tf_op jit(solution)/shard_map/ppermute | solution.py:20
  202.0 10.3 %collective-permute-start.21 = (f32[1,2048]{1,0:T(1,128)S(1)}, f32[1,2048]{1,0:T(1,128)S(1)}, u32[]{:S(2)}, u32[]{:S(2)}) collective-permute-start(f32[1,2048]{1,0:T(1,128)S(1)} %collective-permute-done.19), channel_id=1, source_target_pairs={{0,15},{1,0},{2,1},{3,2},{4,3},{5,4},{6,5},{7,6},{8,7},{9,8},{10,9... | collective-permute-start | bytes 24584 | tf_op jit(solution)/shard_map/ppermute | solution.py:25
  207.1 5.8 %collective-permute-start.22 = (f32[1,2048]{1,0:T(1,128)S(1)}, f32[1,2048]{1,0:T(1,128)S(1)}, u32[]{:S(2)}, u32[]{:S(2)}) collective-permute-start(f32[1,2048]{1,0:T(1,128)S(1)} %collective-permute-done.20), channel_id=1, source_target_pairs={{0,1},{1,2},{2,3},{3,4},{4,5},{5,6},{6,7},{7,8},{8,9},{9,10},{10,1... | collective-permute-start | bytes 24584 | tf_op jit(solution)/shard_map/ppermute | solution.py:20
  (8 other events, 46.2 us)
Sparse Core Ops, SparseCore 0:
  80.7 84.6 all-reduce.61
